TPU v7x, 1024 devices: a whole 8x8x8 slice. The times are simulated.
1024 devices in a mesh: blk: 32 (over z, x_hi), inner: 32 (over y, x_lo, core).
Axes of the slice: x: 8 (x_hi: 4, x_lo: 2; x = x_hi * 2 + x_lo), y: 8, z: 8, core: 2. Of those that a mesh axis runs over, the one named last changes fastest.
Arguments:
- image_student: bfloat16 [229376, 1152], P(('blk', 'inner')), may hold values from -6 to 6
- text_student: bfloat16 [229376, 1152], P(('blk', 'inner')), may hold values from -6 to 6
- image_teacher: bfloat16 [229376, 1152], P(('blk', 'inner')), may hold values from -6 to 6
- text_teacher: bfloat16 [229376, 1152], P(('blk', 'inner')), may hold values from -6 to 6
- pair_ids: int32 [229376], replicated, may hold values from 0 to 28671
Outputs:
- image_grad: bfloat16 [229376, 1152], P(('blk', 'inner'))
- text_grad: bfloat16 [229376, 1152], P(('blk', 'inner'))
Inputs may be any that keep to these rules, and one draw needn't show every extreme that they name: Image row i and text row j form a positive pair exactly when pair_ids[i] == pair_ids[j]; every row is positive with its own text.
All inputs are finite; a program needn't handle non-finite values.
Results may differ from a plain program's by a relative error of at most 0.012.
Values may be sent and summed in bfloat16 or wider, within the bound.
A program may use at most 32 MiB of HBM per device.

v0:
```python
import jax
import jax.numpy as jnp
from jax import lax
from jax.sharding import PartitionSpec as P

WINDOW = 4


logit_gain = 32.0
logit_shift = -2.0


def shifted(block, axis, distance):
    devices = range(lax.axis_size(axis))
    route = [((i - distance) % len(devices), i) for i in devices]
    return lax.ppermute(block, axis, route)


def signal_block(img_s, img_t, ids_img, txt_s, txt_t, ids_txt):
    width = img_s.shape[1]
    student = (
        logit_gain / width * jnp.dot(img_s, txt_s.T, preferred_element_type=jnp.float32)
        + logit_shift
    )
    teacher = (
        logit_gain / width * jnp.dot(img_t, txt_t.T, preferred_element_type=jnp.float32)
        + logit_shift
    )
    same = (ids_img[:, None] == ids_txt[None, :]).astype(jnp.float32)
    target = 0.5 * same + 0.5 * jax.nn.sigmoid(teacher)
    return (jax.nn.sigmoid(student) - target).astype(jnp.bfloat16)


def transpose_product(signal, images):
    return lax.dot_general(
        signal, images, (((0,), (0,)), ((), ())), preferred_element_type=jnp.float32
    )


def local(image_student, text_student, image_teacher, text_teacher, pair_ids):
    rows, width = image_student.shape
    devices = lax.axis_size(("blk", "inner"))
    myself = lax.axis_index(("blk", "inner"))
    image_ids = lax.dynamic_slice_in_dim(pair_ids, myself * rows, rows, 0)
    image_total = jnp.zeros((rows, width), jnp.float32)
    signals = []
    current = (text_student, text_teacher)
    for step in range(WINDOW):
        if step > 0:
            current = shifted((current[0], current[1]), ("blk", "inner"), 1)
        source = (myself - step) % devices
        text_ids = lax.dynamic_slice_in_dim(pair_ids, source * rows, rows, 0)
        signal = signal_block(
            image_student, image_teacher, image_ids, current[0], current[1], text_ids
        )
        image_total = image_total + jnp.dot(signal, current[0], preferred_element_type=jnp.float32)
        signals.append(signal)
    text_total = transpose_product(signals[0], image_student)
    for step in range(1, WINDOW):
        term = transpose_product(signals[step], image_student)
        text_total = text_total + shifted(term, ("blk", "inner"), -step)
    scale = logit_gain / width
    return ((scale * image_total).astype(jnp.bfloat16), (scale * text_total).astype(jnp.bfloat16))


def solution(mesh):
    return jax.shard_map(
        local,
        mesh=mesh,
        in_specs=(
            P(("blk", "inner"), None),
            P(("blk", "inner"), None),
            P(("blk", "inner"), None),
            P(("blk", "inner"), None),
            P(),
        ),
        out_specs=(P(("blk", "inner"), None), P(("blk", "inner"), None)),
        check_vma=False,
    )
```

profile of v0, /device:TPU:1, one launch (start us, length us, event | category | flops | bytes accessed | tf_op | source)
XLA Modules:
  0.0 120.9 jit_solution(16609114560861215688)
XLA Ops:
  0.6 0.0 copy-start
  0.6 4.6 %collective-permute-start.1 = (bf16[224,1152]{1,0:T(8,128)(2,1)}, bf16[224,1152]{1,0:T(8,128)(2,1)S(1)}, u32[]{:S(2)}, u32[]{:S(2)}) collective-permute-start(bf16[224,1152]{1,0:T(8,128)(2,1)} %param.8), channel_id=1, source_target_pairs={{1023,0},{0,1},{1,2},{2,3},{3,4},{4,5},{5,6},{6,7},{7,8},{8,9},{9,... | collective-permute-start | bytes 1548296 | tf_op jit(solution)/shard_map/ppermute | solution.py:16
  5.3 1.9 %collective-permute-start = (bf16[224,1152]{1,0:T(8,128)(2,1)}, bf16[224,1152]{1,0:T(8,128)(2,1)S(1)}, u32[]{:S(2)}, u32[]{:S(2)}) collective-permute-start(bf16[224,1152]{1,0:T(8,128)(2,1)} %param.6), channel_id=1, source_target_pairs={{1023,0},{0,1},{1,2},{2,3},{3,4},{4,5},{5,6},{6,7},{7,8},{8,9},{9,... | collective-permute-start | bytes 1548296 | tf_op jit(solution)/shard_map/ppermute | solution.py:16
  7.3 0.9 fusion.62
  8.2 0.0 copy-start.1
  8.2 1.6 %fusion.18 = f32[224,224]{1,0:T(8,128)S(1)} fusion(bf16[224,1152]{1,0:T(8,128)(2,1)} %param.7, bf16[224,1152]{1,0:T(8,128)(2,1)} %param.8, s32[224]{0:T(256)S(1)} %get-tuple-element.4, s32[224]{0:T(256)S(1)} %get-tuple-element.5), kind=kOutput, calls=%fused_computation.30 | convolution fusion | flops 116057088 | bytes 1234688 | tf_op jit(solution)/shard_map/dot_general | solution.py:26
  9.9 0.0 copy-done
  9.9 0.0 copy-done.1
  9.9 0.0 copy-start.2
  9.9 0.4 fusion.61
  10.3 8.1 %collective-permute-done.1 = bf16[224,1152]{1,0:T(8,128)(2,1)S(1)} collective-permute-done((bf16[224,1152]{1,0:T(8,128)(2,1)}, bf16[224,1152]{1,0:T(8,128)(2,1)S(1)}, u32[]{:S(2)}, u32[]{:S(2)}) %collective-permute-start.1) | collective-permute-done | bytes 516128 | tf_op jit(solution)/shard_map/ppermute | solution.py:16
  18.4 1.9 %collective-permute-start.3 = (bf16[224,1152]{1,0:T(8,128)(2,1)S(1)}, bf16[224,1152]{1,0:T(8,128)(2,1)S(1)}, u32[]{:S(2)}, u32[]{:S(2)}) collective-permute-start(bf16[224,1152]{1,0:T(8,128)(2,1)S(1)} %collective-permute-done.1), channel_id=1, source_target_pairs={{1023,0},{0,1},{1,2},{2,3},{3,4},{4,5},{5,6},{6,7},{7,8},{8,9},{9,... | collective-permute-start | bytes 1548296 | tf_op jit(solution)/shard_map/ppermute | solution.py:16
  20.4 0.0 copy-done.2
  20.4 0.4 fusion.31
  20.8 0.0 collective-permute-done
  20.8 2.1 %collective-permute-start.2 = (bf16[224,1152]{1,0:T(8,128)(2,1)S(1)}, bf16[224,1152]{1,0:T(8,128)(2,1)S(1)}, u32[]{:S(2)}, u32[]{:S(2)}) collective-permute-start(bf16[224,1152]{1,0:T(8,128)(2,1)S(1)} %collective-permute-done), channel_id=1, source_target_pairs={{1023,0},{0,1},{1,2},{2,3},{3,4},{4,5},{5,6},{6,7},{7,8},{8,9},{9,... | collective-permute-start | bytes 1548296 | tf_op jit(solution)/shard_map/ppermute | solution.py:16
  22.9 0.4 fusion.60
  23.3 0.3 fusion.64
  23.6 18.5 %collective-permute-start.6 = (f32[224,1152]{1,0:T(8,128)S(1)}, f32[224,1152]{1,0:T(8,128)S(1)}, u32[]{:S(2)}, u32[]{:S(2)}) collective-permute-start(f32[224,1152]{1,0:T(8,128)S(1)} %fusion.64), channel_id=1, source_target_pairs={{1,0},{2,1},{3,2},{4,3},{5,4},{6,5},{7,6},{8,7},{9,8},{10,9},{11,1... | collective-permute-start | bytes 3096584 | tf_op jit(solution)/shard_map/ppermute | solution.py:16
  42.1 0.0 collective-permute-done.3
  42.1 1.9 %collective-permute-start.5 = (bf16[224,1152]{1,0:T(8,128)(2,1)S(1)}, bf16[224,1152]{1,0:T(8,128)(2,1)S(1)}, u32[]{:S(2)}, u32[]{:S(2)}) collective-permute-start(bf16[224,1152]{1,0:T(8,128)(2,1)S(1)} %collective-permute-done.3), channel_id=1, source_target_pairs={{1023,0},{0,1},{1,2},{2,3},{3,4},{4,5},{5,6},{6,7},{7,8},{8,9},{9,... | collective-permute-start | bytes 1548296 | tf_op jit(solution)/shard_map/ppermute | solution.py:16
  44.1 0.4 fusion.44
  44.5 0.0 collective-permute-done.2
  44.5 1.9 %collective-permute-start.4 = (bf16[224,1152]{1,0:T(8,128)(2,1)S(1)}, bf16[224,1152]{1,0:T(8,128)(2,1)S(1)}, u32[]{:S(2)}, u32[]{:S(2)}) collective-permute-start(bf16[224,1152]{1,0:T(8,128)(2,1)S(1)} %collective-permute-done.2), channel_id=1, source_target_pairs={{1023,0},{0,1},{1,2},{2,3},{3,4},{4,5},{5,6},{6,7},{7,8},{8,9},{9,... | collective-permute-start | bytes 1548296 | tf_op jit(solution)/shard_map/ppermute | solution.py:16
  46.4 0.4 fusion.59
  46.8 0.3 fusion.65
  47.2 17.6 %collective-permute-start.7 = (f32[224,1152]{1,0:T(8,128)S(1)}, f32[224,1152]{1,0:T(8,128)S(1)}, u32[]{:S(2)}, u32[]{:S(2)}) collective-permute-start(f32[224,1152]{1,0:T(8,128)S(1)} %fusion.65), channel_id=1, source_target_pairs={{2,0},{3,1},{4,2},{5,3},{6,4},{7,5},{8,6},{9,7},{10,8},{11,9},{12,... | collective-permute-start | bytes 3096584 | tf_op jit(solution)/shard_map/ppermute | solution.py:16
  64.7 0.0 collective-permute-done.5
  64.7 0.4 fusion.57
  65.1 0.0 collective-permute-done.4
  65.1 0.4 fusion.58
  65.5 0.3 fusion.66
  65.9 9.8 %collective-permute-start.8 = (f32[224,1152]{1,0:T(8,128)S(1)}, f32[224,1152]{1,0:T(8,128)S(1)}, u32[]{:S(2)}, u32[]{:S(2)}) collective-permute-start(f32[224,1152]{1,0:T(8,128)S(1)} %fusion.66), channel_id=1, source_target_pairs={{3,0},{4,1},{5,2},{6,3},{7,4},{8,5},{9,6},{10,7},{11,8},{12,9},{13... | collective-permute-start | bytes 3096584 | tf_op jit(solution)/shard_map/ppermute | solution.py:16
  75.7 0.3 fusion.63
  76.0 0.3 convolution_add_fusion.3
  76.3 0.3 convolution_add_fusion.2
  76.7 1.1 fusion.4
  77.8 0.0 collective-permute-done.6
  77.8 9.5 %collective-permute-done.7 = f32[224,1152]{1,0:T(8,128)S(1)} collective-permute-done((f32[224,1152]{1,0:T(8,128)S(1)}, f32[224,1152]{1,0:T(8,128)S(1)}, u32[]{:S(2)}, u32[]{:S(2)}) %collective-permute-start.7) | collective-permute-done | bytes 1032224 | tf_op jit(solution)/shard_map/ppermute | solution.py:16
  87.3 32.4 %collective-permute-done.8 = f32[224,1152]{1,0:T(8,128)S(1)} collective-permute-done((f32[224,1152]{1,0:T(8,128)S(1)}, f32[224,1152]{1,0:T(8,128)S(1)}, u32[]{:S(2)}, u32[]{:S(2)}) %collective-permute-start.8) | collective-permute-done | bytes 1032224 | tf_op jit(solution)/shard_map/ppermute | solution.py:16
  119.8 1.1 fusion.5
Async XLA Ops:
  0.6 9.2 %copy-start = (bf16[224,1152]{1,0:T(8,128)(2,1)S(1)}, bf16[224,1152]{1,0:T(8,128)(2,1)}, u32[]{:S(2)}) copy-start(bf16[224,1152]{1,0:T(8,128)(2,1)} %param.5) | copy-start | bytes 1548292
  0.6 17.8 %collective-permute-start.1 = (bf16[224,1152]{1,0:T(8,128)(2,1)}, bf16[224,1152]{1,0:T(8,128)(2,1)S(1)}, u32[]{:S(2)}, u32[]{:S(2)}) collective-permute-start(bf16[224,1152]{1,0:T(8,128)(2,1)} %param.8), channel_id=1, source_target_pairs={{1023,0},{0,1},{1,2},{2,3},{3,4},{4,5},{5,6},{6,7},{7,8},{8,9},{9,... | collective-permute-start | bytes 1548296 | tf_op jit(solution)/shard_map/ppermute | solution.py:16
  5.3 15.5 %collective-permute-start = (bf16[224,1152]{1,0:T(8,128)(2,1)}, bf16[224,1152]{1,0:T(8,128)(2,1)S(1)}, u32[]{:S(2)}, u32[]{:S(2)}) collective-permute-start(bf16[224,1152]{1,0:T(8,128)(2,1)} %param.6), channel_id=1, source_target_pairs={{1023,0},{0,1},{1,2},{2,3},{3,4},{4,5},{5,6},{6,7},{7,8},{8,9},{9,... | collective-permute-start | bytes 1548296 | tf_op jit(solution)/shard_map/ppermute | solution.py:16
  8.2 1.7 %copy-start.1 = (bf16[224,1152]{1,0:T(8,128)(2,1)S(1)}, bf16[224,1152]{1,0:T(8,128)(2,1)}, u32[]{:S(2)}) copy-start(bf16[224,1152]{1,0:T(8,128)(2,1)} %param.6) | copy-start | bytes 1548292
  9.9 10.5 %copy-start.2 = (bf16[224,1152]{1,0:T(8,128)(2,1)S(1)}, bf16[224,1152]{1,0:T(8,128)(2,1)}, u32[]{:S(2)}) copy-start(bf16[224,1152]{1,0:T(8,128)(2,1)} %param.7) | copy-start | bytes 1548292
  18.4 23.7 %collective-permute-start.3 = (bf16[224,1152]{1,0:T(8,128)(2,1)S(1)}, bf16[224,1152]{1,0:T(8,128)(2,1)S(1)}, u32[]{:S(2)}, u32[]{:S(2)}) collective-permute-start(bf16[224,1152]{1,0:T(8,128)(2,1)S(1)} %collective-permute-done.1), channel_id=1, source_target_pairs={{1023,0},{0,1},{1,2},{2,3},{3,4},{4,5},{5,6},{6,7},{7,8},{8,9},{9,... | collective-permute-start | bytes 1548296 | tf_op jit(solution)/shard_map/ppermute | solution.py:16
  20.8 23.7 %collective-permute-start.2 = (bf16[224,1152]{1,0:T(8,128)(2,1)S(1)}, bf16[224,1152]{1,0:T(8,128)(2,1)S(1)}, u32[]{:S(2)}, u32[]{:S(2)}) collective-permute-start(bf16[224,1152]{1,0:T(8,128)(2,1)S(1)} %collective-permute-done), channel_id=1, source_target_pairs={{1023,0},{0,1},{1,2},{2,3},{3,4},{4,5},{5,6},{6,7},{7,8},{8,9},{9,... | collective-permute-start | bytes 1548296 | tf_op jit(solution)/shard_map/ppermute | solution.py:16
  23.6 54.1 %collective-permute-start.6 = (f32[224,1152]{1,0:T(8,128)S(1)}, f32[224,1152]{1,0:T(8,128)S(1)}, u32[]{:S(2)}, u32[]{:S(2)}) collective-permute-start(f32[224,1152]{1,0:T(8,128)S(1)} %fusion.64), channel_id=1, source_target_pairs={{1,0},{2,1},{3,2},{4,3},{5,4},{6,5},{7,6},{8,7},{9,8},{10,9},{11,1... | collective-permute-start | bytes 3096584 | tf_op jit(solution)/shard_map/ppermute | solution.py:16
  42.1 22.6 %collective-permute-start.5 = (bf16[224,1152]{1,0:T(8,128)(2,1)S(1)}, bf16[224,1152]{1,0:T(8,128)(2,1)S(1)}, u32[]{:S(2)}, u32[]{:S(2)}) collective-permute-start(bf16[224,1152]{1,0:T(8,128)(2,1)S(1)} %collective-permute-done.3), channel_id=1, source_target_pairs={{1023,0},{0,1},{1,2},{2,3},{3,4},{4,5},{5,6},{6,7},{7,8},{8,9},{9,... | collective-permute-start | bytes 1548296 | tf_op jit(solution)/shard_map/ppermute | solution.py:16
  44.5 20.7 %collective-permute-start.4 = (bf16[224,1152]{1,0:T(8,128)(2,1)S(1)}, bf16[224,1152]{1,0:T(8,128)(2,1)S(1)}, u32[]{:S(2)}, u32[]{:S(2)}) collective-permute-start(bf16[224,1152]{1,0:T(8,128)(2,1)S(1)} %collective-permute-done.2), channel_id=1, source_target_pairs={{1023,0},{0,1},{1,2},{2,3},{3,4},{4,5},{5,6},{6,7},{7,8},{8,9},{9,... | collective-permute-start | bytes 1548296 | tf_op jit(solution)/shard_map/ppermute | solution.py:16
  47.2 40.2 %collective-permute-start.7 = (f32[224,1152]{1,0:T(8,128)S(1)}, f32[224,1152]{1,0:T(8,128)S(1)}, u32[]{:S(2)}, u32[]{:S(2)}) collective-permute-start(f32[224,1152]{1,0:T(8,128)S(1)} %fusion.65), channel_id=1, source_target_pairs={{2,0},{3,1},{4,2},{5,3},{6,4},{7,5},{8,6},{9,7},{10,8},{11,9},{12,... | collective-permute-start | bytes 3096584 | tf_op jit(solution)/shard_map/ppermute | solution.py:16
  65.9 53.9 %collective-permute-start.8 = (f32[224,1152]{1,0:T(8,128)S(1)}, f32[224,1152]{1,0:T(8,128)S(1)}, u32[]{:S(2)}, u32[]{:S(2)}) collective-permute-start(f32[224,1152]{1,0:T(8,128)S(1)} %fusion.66), channel_id=1, source_target_pairs={{3,0},{4,1},{5,2},{6,3},{7,4},{8,5},{9,6},{10,7},{11,8},{12,9},{13... | collective-permute-start | bytes 3096584 | tf_op jit(solution)/shard_map/ppermute | solution.py:16
where the time goes:
time: 121 us
  starting transfers between devices  60.3 us (50%)
  waiting for transfers between devices  50.1 us (41%)
  matrix products  8.58 us (7%)
    ppermute x9, starting transfers between devices, shifted(): return lax.ppermute(block, axis, route)  60.3 us
    ppermute x9, waiting for transfers between devices, shifted(): return lax.ppermute(block, axis, route)  50.1 us
    dot_general x4, matrix products, signal_block(): jnp.dot(img_t, txt_t.T, preferred_element_type=jnp.float32)  2.8 us
  transfers between devices with their start and end apart: 9, of which 3 were waited for; matrix products, arithmetic and copies ran while one was open for 7% of the time, Pallas kernels for 0%

commit v1 on v0

v1 whole, which is shorter than its diff:
```python
import functools

import jax
import jax.numpy as jnp
from jax import lax
from jax.experimental import pallas as pl
from jax.experimental.pallas import tpu as pltpu
from jax.sharding import PartitionSpec as P

MESH = pl.DeviceIdType.MESH
LANES = 128
PARTS = 2

logit_gain = 32.0
logit_shift = -2.0


def kernel(
    n_blk, n_inner, img_s, txt_s, img_t, txt_t, ids, image_grad, text_grad,
    IS, IT, TS, TT, XS, XT, SIG, SIGX, IDS, COL, H_OWN, H_ACC, H_SUM, H1S, H2S, H1R, H2R,
    G_OWN, GS, GR, GXS, GXR, G_OUT, H_OUT,
    load_sem, img_sem, x_sem, p1_send, p1_recv, p2_send, p2_recv, fwd_send,
    h1_sem, h2_sem, g_sem, gx_sem, out_sem,
):
    rows, width = img_s.shape
    part = rows // PARTS
    gain = logit_gain / width
    n_dev = n_blk * n_inner
    blk, inner = lax.axis_index("blk"), lax.axis_index("inner")
    g = blk * n_inner + inner
    core = lax.rem(inner, 2)
    right_x = lax.rem(inner // 2, 2) == 1
    y = inner // 4
    top, bottom = y == n_inner // 4 - 1, y == 0
    c0, c1 = core == 0, core == 1
    no = jnp.logical_not

    has_p2 = c1 & no(bottom)
    forwards = has_p2 & right_x
    sends_p2 = c1 & no(top)
    sends_p1 = no(sends_p2 & right_x)
    gets_x = c1 & ((right_x & top) | (no(right_x) & bottom))
    sends_x = c0 & bottom

    def block(shift):
        return lax.rem(g + shift + n_dev, n_dev)

    def at(shift):
        b = block(shift)
        return (b // n_inner, lax.rem(b, n_inner))

    mate = (blk, inner + 1 - 2 * core)
    after, before, after2, before2 = at(2), at(-2), at(4), at(-4)
    step_up, step_down = at(1), at(-1)

    def piece(r):
        return pl.ds(r * part, part)

    def remote(src, dst, send, recv, to):
        return pltpu.make_async_remote_copy(
            src_ref=src, dst_ref=dst, send_sem=send, recv_sem=recv, device_id=to, device_id_type=MESH
        )

    loads = [
        pltpu.make_async_copy(src, dst, load_sem.at[i])
        for i, (src, dst) in enumerate(
            ((txt_s, TS.at[0]), (img_s, IS.at[0]), (txt_t, TT.at[0]), (img_t, IT.at[0]), (ids, IDS))
        )
    ]
    to_mate = [
        remote(src, dst, img_sem.at[0, i], img_sem.at[1, i], mate)
        for i, (src, dst) in enumerate(((img_s, IS.at[1]), (img_t, IT.at[1])))
    ]
    to_x = [
        remote(src, dst, x_sem.at[0, i], x_sem.at[1, i], step_down)
        for i, (src, dst) in enumerate(((img_s, XS), (img_t, XT)))
    ]
    p1, p2, fwd = {}, {}, {}
    for r in range(PARTS):
        for i, (src, held) in enumerate(((txt_s, TS), (txt_t, TT))):
            k = 2 * r + i
            p1[r, i] = remote(src.at[piece(r)], held.at[1, piece(r)], p1_send.at[k], p1_recv.at[k], after)
            p2[r, i] = remote(src.at[piece(r)], held.at[2, piece(r)], p2_send.at[k], p2_recv.at[k], after2)
            fwd[r, i] = remote(
                held.at[2, piece(r)], held.at[1, piece(r)], fwd_send.at[k], p1_recv.at[k], before
            )
    h1 = [remote(H1S.at[piece(r)], H1R.at[piece(r)], h1_sem.at[0, r], h1_sem.at[1, r], before) for r in range(PARTS)]
    h2 = [remote(H2S.at[piece(r)], H2R.at[piece(r)], h2_sem.at[0, r], h2_sem.at[1, r], before2) for r in range(PARTS)]
    g_copy = remote(GS, GR, g_sem.at[0], g_sem.at[1], mate)
    gx_copy = remote(GXS, GXR, gx_sem.at[0], gx_sem.at[1], step_up)
    g_out = pltpu.make_async_copy(G_OUT, image_grad, out_sem.at[PARTS])
    h_out = [
        pltpu.make_async_copy(H_OUT.at[piece(r)], text_grad.at[piece(r)], out_sem.at[r]) for r in range(PARTS)
    ]

    barrier = pltpu.get_barrier_semaphore()

    def greet(to):
        pl.semaphore_signal(barrier, inc=1, device_id=to, device_id_type=MESH)

    for to in (after, before, mate):
        greet(to)

    @pl.when(c1)
    def _():
        greet(after2)
        greet(before2)

    @pl.when(gets_x)
    def _():
        greet(step_up)

    @pl.when(sends_x)
    def _():
        greet(step_down)

    for copy in loads:
        copy.start()
    peers = 3 + 2 * core + jnp.where(gets_x | sends_x, 1, 0)
    pl.semaphore_wait(barrier, peers)

    @pl.when(sends_p1)
    def _():
        for key in p1:
            p1[key].start()

    @pl.when(sends_p2)
    def _():
        for key in p2:
            p2[key].start()

    for copy in to_mate:
        copy.start()

    @pl.when(sends_x)
    def _():
        for copy in to_x:
            copy.start()

    for copy in loads:
        copy.wait()

    def lane_ids(b):
        start = b * rows
        first = jnp.minimum(start // LANES, IDS.shape[0] - 3)
        offset = start - first * LANES
        line = jnp.concatenate([IDS[pl.ds(first + i, 1), :] for i in range(3)], axis=1)
        line = jnp.broadcast_to(line.astype(jnp.float32), (8, 3 * LANES))
        return pltpu.roll(line, lax.rem(3 * LANES - offset, 3 * LANES), 1)[0:1]

    even = g - core
    own_ids = lane_ids(g)[:, :rows]
    mate_ids = lane_ids(even + 1 - core)[:, :rows]
    x_ids = lane_ids(block(1))[:, :rows]
    for q, b in enumerate((g, block(-2), block(-4))):
        COL[q] = jnp.transpose(jnp.broadcast_to(lane_ids(b)[:, : 2 * LANES], (LANES, 2 * LANES)))

    def nt(a, b):
        return lax.dot_general(a, b, (((1,), (1,)), ((), ())), preferred_element_type=jnp.float32)

    def tn(a, b):
        return lax.dot_general(a, b, (((0,), (0,)), ((), ())), preferred_element_type=jnp.float32)

    def nn(a, b):
        return jnp.dot(a, b, preferred_element_type=jnp.float32)

    def signal(q, r, student_img, teacher_img, img_ids):
        span = pl.ds(0, rows) if r is None else piece(r)
        student = (0.5 * gain) * nt(TS[q, span], student_img[...]) + 0.5 * logit_shift
        teacher = (0.5 * gain) * nt(TT[q, span], teacher_img[...]) + 0.5 * logit_shift
        same = jnp.where(COL[q, span, 0:1] == img_ids, 0.5, 0.0)
        target = same + (0.25 + 0.25 * jnp.tanh(teacher))
        return ((0.5 + 0.5 * jnp.tanh(student)) - target).astype(jnp.bfloat16)

    own = signal(0, None, IS.at[0], IT.at[0], own_ids)
    SIG[0, 0] = own
    H_OWN[...] = nn(own, IS[0])
    for copy in to_mate:
        copy.wait_recv()

    @pl.when(c0)
    def _():
        other = signal(0, None, IS.at[1], IT.at[1], mate_ids)
        SIG[0, 1] = other
        H_OWN[...] += nn(other, IS[1])

    def second(r):
        for i in range(2):
            p2[r, i].wait_recv()

            @pl.when(forwards)
            def _():
                fwd[r, i].start()

        other = signal(2, r, IS.at[1], IT.at[1], mate_ids)
        SIG[2, 1, piece(r)] = other
        H2S[piece(r)] = nn(other, IS[1]).astype(jnp.bfloat16)
        h2[r].start()

    def first(r):
        for i in range(2):
            p1[r, i].wait_recv()
        near = signal(1, r, IS.at[0], IT.at[0], own_ids)
        SIG[1, 0, piece(r)] = near
        other = signal(1, r, IS.at[1], IT.at[1], mate_ids)
        SIG[1, 1, piece(r)] = other
        H_ACC[...] = nn(near, IS[0]) + nn(other, IS[1])

        @pl.when(gets_x)
        def _():
            if r == 0:
                for copy in to_x:
                    copy.wait_recv()
            far = signal(1, r, XS, XT, x_ids)
            SIGX[piece(r)] = far
            H_ACC[...] += nn(far, XS[...])

        H1S[piece(r)] = H_ACC[...].astype(jnp.bfloat16)
        h1[r].start()

    @pl.when(has_p2)
    def _():
        second(0)

    @pl.when(has_p2 & right_x)
    def _():
        second(1)

    first(0)

    @pl.when(has_p2 & no(right_x))
    def _():
        second(1)

    first(1)

    @pl.when(gets_x)
    def _():
        GXS[...] = tn(SIGX[...], TS[1]).astype(jnp.bfloat16)
        gx_copy.start()

    G_OWN[...] = tn(SIG[1, 1], TS[1])

    @pl.when(c0)
    def _():
        G_OWN[...] += tn(SIG[0, 1], TS[0])

    @pl.when(has_p2)
    def _():
        G_OWN[...] += tn(SIG[2, 1], TS[2])

    GS[...] = G_OWN[...].astype(jnp.bfloat16)
    g_copy.start()
    G_OWN[...] = tn(SIG[0, 0], TS[0]) + tn(SIG[1, 0], TS[1])

    @pl.when(sends_x)
    def _():
        gx_copy.wait_recv()
        G_OWN[...] += GXR[...].astype(jnp.float32)

    g_copy.wait_recv()
    G_OUT[...] = (gain * (G_OWN[...] + GR[...].astype(jnp.float32))).astype(jnp.bfloat16)
    g_out.start()

    for r in range(PARTS):
        @pl.when(sends_p2)
        def _():
            h2[r].wait_recv()
            H_OWN[piece(r)] += H2R[piece(r)].astype(jnp.float32)

        h1[r].wait_recv()
        H_OUT[piece(r)] = (gain * (H_OWN[piece(r)] + H1R[piece(r)].astype(jnp.float32))).astype(jnp.bfloat16)
        h_out[r].start()

    for copy in to_mate + h1 + [g_copy]:
        copy.wait_send()

    @pl.when(sends_p1)
    def _():
        for key in p1:
            p1[key].wait_send()

    @pl.when(sends_p2)
    def _():
        for key in p2:
            p2[key].wait_send()

    @pl.when(forwards)
    def _():
        for key in fwd:
            fwd[key].wait_send()

    @pl.when(has_p2)
    def _():
        for copy in h2:
            copy.wait_send()

    @pl.when(sends_x)
    def _():
        for copy in to_x:
            copy.wait_send()

    @pl.when(gets_x)
    def _():
        gx_copy.wait_send()

    for copy in h_out + [g_out]:
        copy.wait()


def local(n_blk, n_inner, image_student, text_student, image_teacher, text_teacher, pair_ids):
    rows, width = image_student.shape
    bf, f32 = jnp.bfloat16, jnp.float32
    VM, DMA = pltpu.VMEM, pltpu.SemaphoreType.DMA
    ids = pair_ids.reshape(-1, LANES)
    part = rows // PARTS
    one = (rows, width)
    return pl.pallas_call(
        functools.partial(kernel, n_blk, n_inner),
        out_shape=(jax.ShapeDtypeStruct(one, bf), jax.ShapeDtypeStruct(one, bf)),
        in_specs=[pl.BlockSpec(memory_space=pl.ANY)] * 5,
        out_specs=(pl.BlockSpec(memory_space=pl.ANY),) * 2,
        scratch_shapes=[
            VM((2, *one), bf), VM((2, *one), bf),
            VM((3, *one), bf), VM((3, *one), bf),
            VM(one, bf), VM(one, bf),
            VM((3, 2, rows, rows), bf), VM((rows, rows), bf),
            VM(ids.shape, jnp.int32), VM((3, 2 * LANES, LANES), f32),
            VM(one, f32), VM((part, width), f32), VM((8, LANES), f32),
            VM(one, bf), VM(one, bf), VM(one, bf), VM(one, bf),
            VM(one, f32), VM(one, bf), VM(one, bf), VM(one, bf), VM(one, bf),
            VM(one, bf), VM(one, bf),
            DMA((5,)), DMA((2, 2)), DMA((2, 2)),
            DMA((2 * PARTS,)), DMA((2 * PARTS,)), DMA((2 * PARTS,)), DMA((2 * PARTS,)), DMA((2 * PARTS,)),
            DMA((2, PARTS)), DMA((2, PARTS)), DMA((2,)), DMA((2,)), DMA((PARTS + 1,)),
        ],
        compiler_params=pltpu.CompilerParams(
            collective_id=0, has_side_effects=True, vmem_limit_bytes=48 << 20
        ),
        name="window_grads",
    )(image_student, text_student, image_teacher, text_teacher, ids)


def solution(mesh):
    both = P(("blk", "inner"), None)
    return jax.shard_map(
        functools.partial(local, mesh.shape["blk"], mesh.shape["inner"]),
        mesh=mesh,
        in_specs=(both, both, both, both, P()),
        out_specs=(both, both),
        check_vma=False,
    )
```

time: 121 us -> 65.3 us (0.54)
  the two profiles are of different devices: /device:TPU:1 before, /device:TPU:2 now
where the time goes in v1:
time: 65.3 us; the launch traced here: 65 us
  Pallas kernels  57.4 us (88%)
  local copies, waits for them, and re-layouts  6.9 us (11%)
    pallas_call x1, Pallas kernels, local(): pl.pallas_call(functools.partial(kernel, n_blk, n_inner), out_shape=(jax....  57.4 us
    unnamed x12, local copies, waits for them, and re-layouts  6.9 us

profile of v1, /device:TPU:2, one launch (start us, length us, event | category | flops | bytes accessed | tf_op | source)
XLA Modules:
  0.0 65.0 jit_solution(1928943219659034239)
XLA Ops:
  0.6 0.0 copy-start
  0.6 1.2 %copy-done = s32[229376]{0:T(1024)S(1)} copy-done((s32[229376]{0:T(1024)S(1)}, s32[229376]{0:T(1024)}, u32[]{:S(2)}) %copy-start) | copy-done | bytes 917528
  1.8 0.0 copy-start.1
  1.8 1.0 %copy-done.1 = bf16[224,1152]{1,0:T(8,128)(2,1)S(1)} copy-done((bf16[224,1152]{1,0:T(8,128)(2,1)S(1)}, bf16[224,1152]{1,0:T(8,128)(2,1)}, u32[]{:S(2)}) %copy-start.1) | copy-done | bytes 516120
  2.9 0.0 copy-start.2
  2.9 1.0 %copy-done.2 = bf16[224,1152]{1,0:T(8,128)(2,1)S(1)} copy-done((bf16[224,1152]{1,0:T(8,128)(2,1)S(1)}, bf16[224,1152]{1,0:T(8,128)(2,1)}, u32[]{:S(2)}) %copy-start.2) | copy-done | bytes 516120
  3.9 0.0 copy-start.3
  3.9 1.0 %copy-done.3 = bf16[224,1152]{1,0:T(8,128)(2,1)S(1)} copy-done((bf16[224,1152]{1,0:T(8,128)(2,1)S(1)}, bf16[224,1152]{1,0:T(8,128)(2,1)}, u32[]{:S(2)}) %copy-start.3) | copy-done | bytes 516120
  4.9 0.0 copy-start.4
  4.9 1.0 %copy-done.4 = bf16[224,1152]{1,0:T(8,128)(2,1)S(1)} copy-done((bf16[224,1152]{1,0:T(8,128)(2,1)S(1)}, bf16[224,1152]{1,0:T(8,128)(2,1)}, u32[]{:S(2)}) %copy-start.4) | copy-done | bytes 516120
  6.0 57.4 %window_grads.1 = (bf16[224,1152]{1,0:T(8,128)(2,1)S(1)}, bf16[224,1152]{1,0:T(8,128)(2,1)S(1)}) custom-call(bf16[224,1152]{1,0:T(8,128)(2,1)S(1)} %copy-done.1, bf16[224,1152]{1,0:T(8,128)(2,1)S(1)} %copy-done.2, bf16[224,1152]{1,0:T(8,128)(2,1)S(1)} %copy-done.3, bf16[224,1152]{1,0:T(8,128)(2,1)S(1)} %copy-done.4, s32[1792,128]{1,0:T(8,128)S(1)} %bitcast.1), custom_call_target="tpu_custom_call" | custom-call | tf_op jit(solution)/shard_map/window_grads/pallas_call | solution.py:318
  63.4 0.8 %copy.9 = bf16[224,1152]{1,0:T(8,128)(2,1)} copy(bf16[224,1152]{1,0:T(8,128)(2,1)S(1)} %get-tuple-element.4) | data formatting | bytes 1032192
  64.2 0.8 %copy.10 = bf16[224,1152]{1,0:T(8,128)(2,1)} copy(bf16[224,1152]{1,0:T(8,128)(2,1)S(1)} %get-tuple-element.5) | data formatting | bytes 1032192
Async XLA Ops:
  0.6 1.2 %copy-start = (s32[229376]{0:T(1024)S(1)}, s32[229376]{0:T(1024)}, u32[]{:S(2)}) copy-start(s32[229376]{0:T(1024)} %param.9) | copy-start | bytes 2752516
  1.8 1.0 %copy-start.1 = (bf16[224,1152]{1,0:T(8,128)(2,1)S(1)}, bf16[224,1152]{1,0:T(8,128)(2,1)}, u32[]{:S(2)}) copy-start(bf16[224,1152]{1,0:T(8,128)(2,1)} %img_s.1) | copy-start | bytes 1548292
  2.9 1.0 %copy-start.2 = (bf16[224,1152]{1,0:T(8,128)(2,1)S(1)}, bf16[224,1152]{1,0:T(8,128)(2,1)}, u32[]{:S(2)}) copy-start(bf16[224,1152]{1,0:T(8,128)(2,1)} %txt_s.1) | copy-start | bytes 1548292
  3.9 1.0 %copy-start.3 = (bf16[224,1152]{1,0:T(8,128)(2,1)S(1)}, bf16[224,1152]{1,0:T(8,128)(2,1)}, u32[]{:S(2)}) copy-start(bf16[224,1152]{1,0:T(8,128)(2,1)} %img_t.1) | copy-start | bytes 1548292
  4.9 1.0 %copy-start.4 = (bf16[224,1152]{1,0:T(8,128)(2,1)S(1)}, bf16[224,1152]{1,0:T(8,128)(2,1)}, u32[]{:S(2)}) copy-start(bf16[224,1152]{1,0:T(8,128)(2,1)} %txt_t.1) | copy-start | bytes 1548292
